TPU v7x, 512 devices: a whole 4x8x8 slice. The times are simulated.
512 devices in a mesh: row: 8 (over z), col: 16 (over y_hi, x, core), kpart: 4 (over y_lo).
Axes of the slice: x: 4, y: 8 (y_hi: 2, y_lo: 4; y = y_hi * 4 + y_lo), z: 8, core: 2. Of those that a mesh axis runs over, the one named last changes fastest.
Arguments:
- left_cyclic: float32 [2048, 8192], P(('kpart', 'col'), 'row'), may hold values from -6 to 6
- right_cyclic: float32 [2048, 16384], P(('kpart', 'row'), 'col'), may hold values from -0.125 to 0.125
Outputs:
- product: float32 [8192, 16384], P(('row', 'kpart'), 'col')
All inputs are finite; a program needn't handle non-finite values.
Results may differ from a plain program's by a relative error of at most 0.00007.
Values sent between devices are 32-bit elements; how exact they have to be, the bound alone decides.
No kernel may reach another device: no remote copies, remote signals or barrier semaphores. Data moves between devices by JAX's collectives and lax.ppermute only.
A program may use at most 64 MiB of HBM per device.

v0:
```python
import jax
import jax.numpy as jnp
from jax import lax
from jax.sharding import PartitionSpec as P

NB = 64


def contract(left_part, right_part):
    return lax.dot_general(
        left_part,
        right_part,
        (((0,), (0,)), ((), ())),
        precision=lax.Precision.HIGHEST,
        preferred_element_type=jnp.float32,
    )


def shards(left_cyclic, right_cyclic):
    row_count = lax.axis_size("row")
    column_count = lax.axis_size("col")
    slab_left, local_rows = left_cyclic.shape
    group_left = local_rows // (NB * row_count)
    shaped_left = left_cyclic.reshape(slab_left, row_count, group_left, 1, NB)
    moved_left = lax.all_to_all(shaped_left, "row", split_axis=1, concat_axis=3, tiled=True)
    band_left = moved_left.reshape(slab_left, local_rows)
    left_band = lax.all_gather(band_left, "col", axis=0, tiled=True)
    slab_right, local_cols = right_cyclic.shape
    group_right = local_cols // (NB * column_count)
    shaped_right = right_cyclic.reshape(slab_right, column_count, group_right, 1, NB)
    moved_right = lax.all_to_all(shaped_right, "col", split_axis=1, concat_axis=3, tiled=True)
    band_right = moved_right.reshape(slab_right, local_cols)
    right_band = lax.all_gather(band_right, "row", axis=0, tiled=True)
    return lax.psum_scatter(
        contract(left_band, right_band), "kpart", scatter_dimension=0, tiled=True
    )


def solution(mesh):
    placed = (P(("kpart", "col"), "row"), P(("kpart", "row"), "col"))
    return jax.shard_map(
        shards, mesh=mesh, in_specs=placed, out_specs=P(("row", "kpart"), "col"), check_vma=False
    )
```

profile of v0, /device:TPU:57, one launch (start us, length us, event | category | flops | bytes accessed | tf_op | source)
XLA Modules:
  0.0 246.7 jit_solution(4141008044242358849)
XLA Ops:
  6.5 0.0 all-gather.5.cloned.1.call-start
  6.5 1.1 reshape.19
  7.6 0.2 copy.11
  7.8 0.3 reshape.23
  8.1 0.0 copy-start
  8.2 16.5 %all_to_all.24 = f32[16,1,4096]{2,1,0:T(1,128)S(1)} all-to-all(f32[16,1,4096]{2,1,0:T(1,128)S(1)} %reshape.23), channel_id=1, replica_groups=mesh['row'=8,'col'=16,'kpart'=4] {'col'}, dimensions={0} | all-to-all | bytes 524288 | tf_op jit(solution)/shard_map/all_to_all | solution.py:31
  24.7 0.5 broadcast
  25.2 1.2 reduce.1
  26.5 0.2 reshape.24
  26.7 0.3 copy.8
  27.0 0.9 reshape.20
  27.9 0.0 all-gather.5.cloned.1.call-update
  27.9 0.0 all-gather.3.cloned.1.call-start
  28.0 0.0 copy-done
  28.0 0.2 reshape.17
  28.2 0.1 copy.12
  28.3 0.3 reshape.21
  28.5 17.6 %all_to_all.25 = f32[8,1,4096]{2,1,0:T(1,128)S(1)} all-to-all(f32[8,1,4096]{2,1,0:T(1,128)S(1)} %reshape.21), channel_id=1, replica_groups=mesh['row'=8,'col'=16,'kpart'=4] {'row'}, dimensions={0} | all-to-all | bytes 262144 | tf_op jit(solution)/shard_map/all_to_all | solution.py:25
  46.1 0.9 reduce
  47.1 0.2 reshape.22
  47.3 0.2 copy.6
  47.5 0.8 reshape.18
  48.2 0.0 all-gather.3.cloned.1.call-update
  48.3 0.0 reduce-scatter.2.cloned.1.call-start
  48.3 25.2 %all-gather.5.cloned.1.call-done = f32[512,1024]{1,0:T(8,128)} async-done(((f32[64,1024]{1,0:T(8,128)}), f32[512,1024]{1,0:T(8,128)}) %all-gather.5.cloned.1.call-update) | async-done | bytes 2097168 | tf_op jit(solution)/shard_map/all_gather | solution.py:33
  73.5 68.3 %all-gather.3.cloned.1.call-done = f32[512,1024]{1,0:T(8,128)} async-done(((f32[32,1024]{1,0:T(8,128)}), f32[512,1024]{1,0:T(8,128)}) %all-gather.3.cloned.1.call-update) | async-done | bytes 2097168 | tf_op jit(solution)/shard_map/all_gather | solution.py:27
  141.8 10.2 %fusion = f32[1024,1024]{1,0:T(8,128)} fusion(f32[512,1024]{1,0:T(8,128)} %all-gather.3.cloned.1.call-done, f32[512,1024]{1,0:T(8,128)} %all-gather.5.cloned.1.call-done), kind=kOutput, calls=%fused_computation.3 | convolution fusion | flops 6442450944 | bytes 8388608 | tf_op jit(solution)/shard_map/dot_general | solution.py:10
  152.0 0.0 reduce-scatter.2.cloned.1.call-update
  152.0 88.2 %reduce-scatter.2.cloned.1.call-done = f32[256,1024]{1,0:T(8,128)} async-done(((f32[1024,1024]{1,0:T(8,128)}), f32[256,1024]{1,0:T(8,128)}) %reduce-scatter.2.cloned.1.call-update) | async-done | bytes 1048592 | tf_op jit(solution)/shard_map/reduce_scatter | solution.py:34
  (1 shorter events, 0.0 us)
Async XLA Ops:
  6.5 66.9 %all-gather.5.cloned.1.call-start = ((), (), s32[]{:S(2)}) async-start(), calls=%async_computation.4 | async-start | bytes 2359296 | tf_op jit(solution)/shard_map/all_gather | solution.py:33
  8.1 19.8 %copy-start = (f32[32,1024]{1,0:T(8,128)S(1)}, f32[32,1024]{1,0:T(8,128)}, u32[]{:S(2)}) copy-start(f32[32,1024]{1,0:T(8,128)} %param.2) | copy-start | bytes 393220
  27.9 113.9 %all-gather.3.cloned.1.call-start = ((), (), s32[]{:S(2)}) async-start(), calls=%async_computation.3 | async-start | bytes 2228224 | tf_op jit(solution)/shard_map/all_gather | solution.py:27
  48.3 191.9 %reduce-scatter.2.cloned.1.call-start = ((), (), s32[]{:S(2)}) async-start(), calls=%async_computation.5 | async-start | bytes 5242880 | tf_op jit(solution)/shard_map/reduce_scatter | solution.py:34
Sparse Core Ops, SparseCore 0:
  28.0 45.4 all-gather.4
  76.8 64.9 all-gather.2
  152.1 88.0 reduce-scatter.1
where the time goes:
time: 247 us
  waiting for transfers between devices  182 us (74%)
  blocking collectives  34.1 us (14%)
  between operations  13.2 us (5%)
  matrix products  10.2 us (4%)
  local copies, waits for them, and re-layouts  5.21 us (2%)
    reduce_scatter x1, waiting for transfers between devices, shards(): lax.psum_scatter(contract(left_band, right_band), 'kpart', scatter_dimens...  88.2 us
    all_gather x1, waiting for transfers between devices, shards(): left_band = lax.all_gather(band_left, 'col', axis=0, tiled=True)  68.3 us
    all_gather x1, waiting for transfers between devices, shards(): right_band = lax.all_gather(band_right, 'row', axis=0, tiled=True)  25.2 us
    all_to_all x1, blocking collectives, shards(): lax.all_to_all(shaped_left, 'row', split_axis=1, concat_axis=3, tiled=True)  17.6 us
    all_to_all x1, blocking collectives, shards(): lax.all_to_all(shaped_right, 'col', split_axis=1, concat_axis=3, tiled=True)  16.5 us
    dot_general x1, matrix products, contract(): lax.dot_general(left_part, right_part, (((0,), (0,)), ((), ())), precisio...  10.2 us
  transfers between devices with their start and end apart: 3, of which 3 were waited for; matrix products, arithmetic and copies ran while one was open for 1% of the time, Pallas kernels for 0%

commit v1 on v0

--- a/solution.py
+++ b/solution.py
@@ -4,6 +4,24 @@
 from jax.sharding import PartitionSpec as P
 
 NB = 64
+
+
+def gather_around(array, axis, dim):
+    ways, here, step = (lax.axis_size(axis), lax.axis_index(axis), array.shape[dim])
+    lengths = [n * ways if d == dim else n for d, n in enumerate(array.shape)]
+    full = lax.dynamic_update_slice_in_dim(
+        jnp.zeros(lengths, array.dtype), array, here * step, axis=dim
+    )
+    going_up = going_down = array
+    for far in range(1, ways // 2 + 1):
+        going_up = lax.ppermute(going_up, axis, [(d, (d + 1) % ways) for d in range(ways)])
+        full = lax.dynamic_update_slice_in_dim(full, going_up, (here - far) % ways * step, axis=dim)
+        if 2 * far < ways:
+            going_down = lax.ppermute(going_down, axis, [(d, (d - 1) % ways) for d in range(ways)])
+            full = lax.dynamic_update_slice_in_dim(
+                full, going_down, (here + far) % ways * step, axis=dim
+            )
+    return full
 
 
 def contract(left_part, right_part):
@@ -30,7 +48,7 @@
     shaped_right = right_cyclic.reshape(slab_right, column_count, group_right, 1, NB)
     moved_right = lax.all_to_all(shaped_right, "col", split_axis=1, concat_axis=3, tiled=True)
     band_right = moved_right.reshape(slab_right, local_cols)
-    right_band = lax.all_gather(band_right, "row", axis=0, tiled=True)
+    right_band = gather_around(band_right, "row", 0)
     return lax.psum_scatter(
         contract(left_band, right_band), "kpart", scatter_dimension=0, tiled=True
     )

time: 247 us -> 198 us (0.80)
  waiting for transfers between devices: 182 us -> 107 us
  starting transfers between devices: 0.09 us -> 21.4 us
    all_gather x1, waiting for transfers between devices: 68.3 us -> 0.57 us  [shards(): left_band = lax.all_gather(band_left, 'col', axis=0, tiled=True)]
    all_gather x1 -> x0, waiting for transfers between devices: 25.2 us -> none  [shards(): right_band = lax.all_gather(band_right, 'row', axis=0, tiled=True)]
    ppermute x0 -> x7, starting transfers between devices: none -> 21.4 us  [the longest x3 13.7 us: gather_around(): lax.ppermute(going_down, axis, [(d, (d - 1) % ways) for d in range(ways)])]
    ppermute x0 -> x7, waiting for transfers between devices: none -> 17 us  [the longest x4 17 us: gather_around(): lax.ppermute(going_up, axis, [(d, (d + 1) % ways) for d in range(ways)])]
    reduce_scatter x0 -> x1, local copies, waits for them, and re-layouts: none -> 2.53 us  [shards(): lax.psum_scatter(contract(left_band, right_band), 'kpart', scatter_dimens...]
  transfers between devices with their start and end apart: 3 -> 9, of which waited for: 3 -> 6; matrix products, arithmetic and copies ran while one was open for 1% -> 1% of each run, Pallas kernels for 0% -> 0%
where the time goes in v1:
time: 198 us; the launch traced here: 197 us
  waiting for transfers between devices  107 us (54%)
  blocking collectives  36.2 us (18%)
  starting transfers between devices  21.4 us (11%)
  between operations  13.8 us (7%)
  matrix products  9.51 us (5%)
  local copies, waits for them, and re-layouts  7.46 us (4%)
  other arithmetic  2.04 us (1%)
    reduce_scatter x1, waiting for transfers between devices, shards(): lax.psum_scatter(contract(left_band, right_band), 'kpart', scatter_dimens...  89.1 us
    all_to_all x1, blocking collectives, shards(): lax.all_to_all(shaped_right, 'col', split_axis=1, concat_axis=3, tiled=True)  18.6 us
    all_to_all x1, blocking collectives, shards(): lax.all_to_all(shaped_left, 'row', split_axis=1, concat_axis=3, tiled=True)  17.6 us
    ppermute x4, waiting for transfers between devices, gather_around(): lax.ppermute(going_up, axis, [(d, (d + 1) % ways) for d in range(ways)])  17 us
    ppermute x3, starting transfers between devices, gather_around(): lax.ppermute(going_down, axis, [(d, (d - 1) % ways) for d in range(ways)])  13.7 us
    dot_general x1, matrix products, contract(): lax.dot_general(left_part, right_part, (((0,), (0,)), ((), ())), precisio...  9.51 us
    ppermute x4, starting transfers between devices, gather_around(): lax.ppermute(going_up, axis, [(d, (d + 1) % ways) for d in range(ways)])  7.65 us
  transfers between devices with their start and end apart: 9, of which 6 were waited for; matrix products, arithmetic and copies ran while one was open for 1% of the time, Pallas kernels for 0%

profile of v1, /device:TPU:57, one launch (start us, length us, event | category | flops | bytes accessed | tf_op | source)
XLA Modules:
  0.0 197.1 jit_solution(11307466373840043665)
XLA Ops:
  6.5 1.1 reshape.19
  7.8 0.3 reshape.23
  8.1 17.6 %all_to_all.24 = f32[8,1,4096]{2,1,0:T(1,128)S(1)} all-to-all(f32[8,1,4096]{2,1,0:T(1,128)S(1)} %reshape.23), channel_id=1, replica_groups=mesh['row'=8,'col'=16,'kpart'=4] {'row'}, dimensions={0} | all-to-all | bytes 262144 | tf_op jit(solution)/shard_map/all_to_all | solution.py:43
  25.7 0.5 broadcast.7
  26.2 0.9 reduce.1
  27.0 0.2 reshape.24
  27.3 0.2 copy.11
  27.4 0.8 reshape.20
  28.3 0.1 reshape.17
  28.4 0.2 copy.15
  28.6 0.3 reshape.21
  28.9 18.6 %all_to_all.25 = f32[16,1,4096]{2,1,0:T(1,128)S(1)} all-to-all(f32[16,1,4096]{2,1,0:T(1,128)S(1)} %reshape.21), channel_id=1, replica_groups=mesh['row'=8,'col'=16,'kpart'=4] {'col'}, dimensions={0} | all-to-all | bytes 524288 | tf_op jit(solution)/shard_map/all_to_all | solution.py:49
  47.6 1.2 reduce
  48.8 0.2 reshape.22
  49.0 0.3 copy.9
  49.3 0.2 reshape.18
  49.5 1.9 collective-permute-start
  51.4 4.6 %collective-permute-start.1 = (f32[64,1024]{1,0:T(8,128)S(1)}, f32[64,1024]{1,0:T(8,128)S(1)}, u32[]{:S(2)}, u32[]{:S(2)}) collective-permute-start(f32[64,1024]{1,0:T(8,128)S(1)} %reshape.18), channel_id=1, source_target_pairs={{0,448},{64,0},{128,64},{192,128},{256,192},{320,256},{384,320},{4... | collective-permute-start | bytes 786440 | tf_op jit(solution)/shard_map/ppermute | solution.py:20
  56.0 4.6 %collective-permute-done = f32[64,1024]{1,0:T(8,128)S(1)} collective-permute-done((f32[64,1024]{1,0:T(8,128)S(1)}, f32[64,1024]{1,0:T(8,128)S(1)}, u32[]{:S(2)}, u32[]{:S(2)}) %collective-permute-start) | collective-permute-done | bytes 262176 | tf_op jit(solution)/shard_map/ppermute | solution.py:17
  60.6 1.9 collective-permute-start.2
  62.7 4.6 %collective-permute-start.3 = (f32[64,1024]{1,0:T(8,128)S(1)}, f32[64,1024]{1,0:T(8,128)S(1)}, u32[]{:S(2)}, u32[]{:S(2)}) collective-permute-start(f32[64,1024]{1,0:T(8,128)S(1)} %collective-permute-done.1), channel_id=1, source_target_pairs={{0,448},{64,0},{128,64},{192,128},{256,192},{320,256},{384,320},{4... | collective-permute-start | bytes 786440 | tf_op jit(solution)/shard_map/ppermute | solution.py:20
  67.3 0.2 broadcast_in_dim.3
  67.5 3.3 %collective-permute-done.2 = f32[64,1024]{1,0:T(8,128)S(1)} collective-permute-done((f32[64,1024]{1,0:T(8,128)S(1)}, f32[64,1024]{1,0:T(8,128)S(1)}, u32[]{:S(2)}, u32[]{:S(2)}) %collective-permute-start.2) | collective-permute-done | bytes 262176 | tf_op jit(solution)/shard_map/ppermute | solution.py:17
  70.9 1.9 collective-permute-start.4
  72.9 4.6 %collective-permute-start.5 = (f32[64,1024]{1,0:T(8,128)S(1)}, f32[64,1024]{1,0:T(8,128)S(1)}, u32[]{:S(2)}, u32[]{:S(2)}) collective-permute-start(f32[64,1024]{1,0:T(8,128)S(1)} %collective-permute-done.3), channel_id=1, source_target_pairs={{0,448},{64,0},{128,64},{192,128},{256,192},{320,256},{384,320},{4... | collective-permute-start | bytes 786440 | tf_op jit(solution)/shard_map/ppermute | solution.py:20
  77.5 2.7 %collective-permute-done.4 = f32[64,1024]{1,0:T(8,128)S(1)} collective-permute-done((f32[64,1024]{1,0:T(8,128)S(1)}, f32[64,1024]{1,0:T(8,128)S(1)}, u32[]{:S(2)}, u32[]{:S(2)}) %collective-permute-start.4) | collective-permute-done | bytes 262176 | tf_op jit(solution)/shard_map/ppermute | solution.py:17
  80.2 1.9 collective-permute-start.6
  82.2 6.3 %collective-permute-done.6 = f32[64,1024]{1,0:T(8,128)S(1)} collective-permute-done((f32[64,1024]{1,0:T(8,128)S(1)}, f32[64,1024]{1,0:T(8,128)S(1)}, u32[]{:S(2)}, u32[]{:S(2)}) %collective-permute-start.6) | collective-permute-done | bytes 262176 | tf_op jit(solution)/shard_map/ppermute | solution.py:17
  88.5 0.6 all-gather.2.cloned.1.call-done
  89.1 9.5 %convolution_bitcast_fusion = f32[1024,1024]{0,1:T(8,128)} fusion(f32[512,1024]{1,0:T(8,128)S(1)} %constant_dynamic-update-slice_fusion, f32[512,1024]{1,0:T(8,128)} %all-gather.2.cloned.1.call-done), kind=kOutput, calls=%fused_computation | convolution fusion | flops 6442450944 | bytes 8388608 | tf_op jit(solution)/shard_map/dot_general | solution.py:28
  98.6 89.1 %reduce-scatter.2.cloned.1.call-done = f32[256,1024]{0,1:T(8,128)} async-done(((f32[1024,1024]{0,1:T(8,128)}), f32[256,1024]{0,1:T(8,128)}) %reduce-scatter.2.cloned.1.call-update) | async-done | bytes 1048592 | tf_op jit(solution)/shard_map/reduce_scatter | solution.py:52
  187.7 2.5 %copy.12 = f32[256,1024]{1,0:T(8,128)} copy(f32[256,1024]{0,1:T(8,128)} %reduce-scatter.2.cloned.1.call-done) | data formatting | bytes 2097152 | tf_op jit(solution)/shard_map/reduce_scatter | solution.py:52
  (19 shorter events, 0.4 us)
Async XLA Ops:
  6.5 21.7 %copy-start = (f32[64,1024]{1,0:T(8,128)S(1)}, f32[64,1024]{1,0:T(8,128)}, u32[]{:S(2)}) copy-start(f32[64,1024]{1,0:T(8,128)} %param.3) | copy-start | bytes 786436
  6.5 82.6 %all-gather.2.cloned.1.call-start = ((), (), s32[]{:S(2)}) async-start(), calls=%async_computation.3 | async-start | bytes 2228224 | tf_op jit(solution)/shard_map/all_gather | solution.py:45
  28.2 159.5 %reduce-scatter.2.cloned.1.call-start = ((), (), s32[]{:S(2)}) async-start(), calls=%async_computation.4 | async-start | bytes 5242880 | tf_op jit(solution)/shard_map/reduce_scatter | solution.py:52
  49.5 11.1 %collective-permute-start = (f32[64,1024]{1,0:T(8,128)S(1)}, f32[64,1024]{1,0:T(8,128)S(1)}, u32[]{:S(2)}, u32[]{:S(2)}) collective-permute-start(f32[64,1024]{1,0:T(8,128)S(1)} %reshape.18), channel_id=1, source_target_pairs={{0,64},{64,128},{128,192},{192,256},{256,320},{320,384},{384,448},... | collective-permute-start | bytes 786440 | tf_op jit(solution)/shard_map/ppermute | solution.py:17
  51.4 11.3 %collective-permute-start.1 = (f32[64,1024]{1,0:T(8,128)S(1)}, f32[64,1024]{1,0:T(8,128)S(1)}, u32[]{:S(2)}, u32[]{:S(2)}) collective-permute-start(f32[64,1024]{1,0:T(8,128)S(1)} %reshape.18), channel_id=1, source_target_pairs={{0,448},{64,0},{128,64},{192,128},{256,192},{320,256},{384,320},{4... | collective-permute-start | bytes 786440 | tf_op jit(solution)/shard_map/ppermute | solution.py:20
  60.6 10.3 %collective-permute-start.2 = (f32[64,1024]{1,0:T(8,128)S(1)}, f32[64,1024]{1,0:T(8,128)S(1)}, u32[]{:S(2)}, u32[]{:S(2)}) collective-permute-start(f32[64,1024]{1,0:T(8,128)S(1)} %collective-permute-done), channel_id=1, source_target_pairs={{0,64},{64,128},{128,192},{192,256},{256,320},{320,384},{384,448},... | collective-permute-start | bytes 786440 | tf_op jit(solution)/shard_map/ppermute | solution.py:17
  62.7 10.2 %collective-permute-start.3 = (f32[64,1024]{1,0:T(8,128)S(1)}, f32[64,1024]{1,0:T(8,128)S(1)}, u32[]{:S(2)}, u32[]{:S(2)}) collective-permute-start(f32[64,1024]{1,0:T(8,128)S(1)} %collective-permute-done.1), channel_id=1, source_target_pairs={{0,448},{64,0},{128,64},{192,128},{256,192},{320,256},{384,320},{4... | collective-permute-start | bytes 786440 | tf_op jit(solution)/shard_map/ppermute | solution.py:20
  70.9 9.3 %collective-permute-start.4 = (f32[64,1024]{1,0:T(8,128)S(1)}, f32[64,1024]{1,0:T(8,128)S(1)}, u32[]{:S(2)}, u32[]{:S(2)}) collective-permute-start(f32[64,1024]{1,0:T(8,128)S(1)} %collective-permute-done.2), channel_id=1, source_target_pairs={{0,64},{64,128},{128,192},{192,256},{256,320},{320,384},{384,448},... | collective-permute-start | bytes 786440 | tf_op jit(solution)/shard_map/ppermute | solution.py:17
  72.9 9.3 %collective-permute-start.5 = (f32[64,1024]{1,0:T(8,128)S(1)}, f32[64,1024]{1,0:T(8,128)S(1)}, u32[]{:S(2)}, u32[]{:S(2)}) collective-permute-start(f32[64,1024]{1,0:T(8,128)S(1)} %collective-permute-done.3), channel_id=1, source_target_pairs={{0,448},{64,0},{128,64},{192,128},{256,192},{320,256},{384,320},{4... | collective-permute-start | bytes 786440 | tf_op jit(solution)/shard_map/ppermute | solution.py:20
  80.2 8.3 %collective-permute-start.6 = (f32[64,1024]{1,0:T(8,128)S(1)}, f32[64,1024]{1,0:T(8,128)S(1)}, u32[]{:S(2)}, u32[]{:S(2)}) collective-permute-start(f32[64,1024]{1,0:T(8,128)S(1)} %collective-permute-done.4), channel_id=1, source_target_pairs={{0,64},{64,128},{128,192},{192,256},{256,320},{320,384},{384,448},... | collective-permute-start | bytes 786440 | tf_op jit(solution)/shard_map/ppermute | solution.py:17
Sparse Core Ops, SparseCore 0:
  28.4 60.7 all-gather.1
  98.8 88.9 reduce-scatter.1

commit v2 on v0

--- a/solution.py
+++ b/solution.py
@@ -24,7 +24,9 @@
     shaped_left = left_cyclic.reshape(slab_left, row_count, group_left, 1, NB)
     moved_left = lax.all_to_all(shaped_left, "row", split_axis=1, concat_axis=3, tiled=True)
     band_left = moved_left.reshape(slab_left, local_rows)
-    left_band = lax.all_gather(band_left, "col", axis=0, tiled=True)
+    left_band = jnp.concatenate(
+        lax.all_to_all(jnp.stack([band_left] * lax.axis_size("col")), "col", 0, 0), axis=0
+    )
     slab_right, local_cols = right_cyclic.shape
     group_right = local_cols // (NB * column_count)
     shaped_right = right_cyclic.reshape(slab_right, column_count, group_right, 1, NB)

time: 247 us -> 206 us (0.83)
  waiting for transfers between devices: 182 us -> 141 us
  blocking collectives: 34.1 us -> 0 us
  starting transfers between devices: 0.09 us -> 30.8 us
  local copies, waits for them, and re-layouts: 5.21 us -> 8.43 us
    all_gather x1 -> x0, waiting for transfers between devices: 68.3 us -> none  [shards(): left_band = lax.all_gather(band_left, 'col', axis=0, tiled=True)]
    all_to_all x2 -> x0, blocking collectives: 34.1 us -> none  [the longest x1 17.6 us: shards(): lax.all_to_all(shaped_left, 'row', split_axis=1, concat_axis=3, tiled=True)]
    all_to_all x0 -> x3, starting transfers between devices: none -> 30.8 us  [the longest x1 11.6 us: shards(): lax.all_to_all(shaped_right, 'col', split_axis=1, concat_axis=3, tiled=True)]
    all_gather x1, waiting for transfers between devices: 25.2 us -> 37.9 us  [shards(): right_band = lax.all_gather(band_right, 'row', axis=0, tiled=True)]
    all_to_all x0 -> x3, waiting for transfers between devices: none -> 10.1 us  [the longest x1 5.47 us: shards(): lax.all_to_all(shaped_left, 'row', split_axis=1, concat_axis=3, tiled=True)]
    reduce_scatter x1, waiting for transfers between devices: 88.2 us -> 93.3 us  [shards(): lax.psum_scatter(contract(left_band, right_band), 'kpart', scatter_dimens...]
  transfers between devices with their start and end apart: 3 -> 5, of which waited for: 3 -> 4; matrix products, arithmetic and copies ran while one was open for 1% -> 3% of each run, Pallas kernels for 0% -> 0%
where the time goes in v2:
time: 206 us
  waiting for transfers between devices  141 us (68%)
  starting transfers between devices  30.8 us (15%)
  between operations  13.5 us (7%)
  matrix products  9.5 us (5%)
  local copies, waits for them, and re-layouts  8.43 us (4%)
  other arithmetic  2.16 us (1%)
    reduce_scatter x1, waiting for transfers between devices, shards(): lax.psum_scatter(contract(left_band, right_band), 'kpart', scatter_dimens...  93.3 us
    all_gather x1, waiting for transfers between devices, shards(): right_band = lax.all_gather(band_right, 'row', axis=0, tiled=True)  37.9 us
    all_to_all x1, starting transfers between devices, shards(): lax.all_to_all(shaped_right, 'col', split_axis=1, concat_axis=3, tiled=True)  11.6 us
    all_to_all x1, starting transfers between devices, shards(): lax.all_to_all(shaped_left, 'row', split_axis=1, concat_axis=3, tiled=True)  10 us
    dot_general x1, matrix products, contract(): lax.dot_general(left_part, right_part, (((0,), (0,)), ((), ())), precisio...  9.5 us
    all_to_all x1, starting transfers between devices, shards(): lax.all_to_all(jnp.stack([band_left] * lax.axis_size('col')), 'col', 0, 0)  9.12 us
    all_to_all x1, waiting for transfers between devices, shards(): lax.all_to_all(shaped_left, 'row', split_axis=1, concat_axis=3, tiled=True)  5.47 us
    all_to_all x1, waiting for transfers between devices, shards(): lax.all_to_all(shaped_right, 'col', split_axis=1, concat_axis=3, tiled=True)  4.58 us
  transfers between devices with their start and end apart: 5, of which 4 were waited for; matrix products, arithmetic and copies ran while one was open for 3% of the time, Pallas kernels for 0%

profile of v2, /device:TPU:57, one launch (start us, length us, event | category | flops | bytes accessed | tf_op | source)
XLA Modules:
  0.0 205.7 jit_solution(1955868504121492220)
XLA Ops:
  6.5 1.1 reshape.19
  7.6 0.1 copy.12
  7.7 0.9 reshape.23
  8.6 10.0 %all-to-all-start = ((f32[8,1,4096]{2,1,0:T(1,128)}), f32[8,1,4096]{2,1,0:T(1,128)S(1)}, u32[]{:S(2)}, u32[]{:S(2)}) async-start(f32[8,1,4096]{2,1,0:T(1,128)} %reshape.23), calls=%async_computation | async-start | bytes 262144 | tf_op jit(solution)/shard_map/all_to_all | solution.py:25
  18.7 1.1 reshape.21
  19.8 0.2 copy.11
  20.0 1.0 reshape.25
  21.0 5.5 %all-to-all-done = f32[8,1,4096]{2,1,0:T(1,128)S(1)} async-done(((f32[8,1,4096]{2,1,0:T(1,128)}), f32[8,1,4096]{2,1,0:T(1,128)S(1)}, u32[]{:S(2)}, u32[]{:S(2)}) %all-to-all-start) | async-done | bytes 131104 | tf_op jit(solution)/shard_map/all_to_all | solution.py:25
  26.5 11.6 %all-to-all-start.2 = ((f32[16,1,4096]{2,1,0:T(1,128)}), f32[16,1,4096]{2,1,0:T(1,128)S(1)}, u32[]{:S(2)}, u32[]{:S(2)}) async-start(f32[16,1,4096]{2,1,0:T(1,128)} %reshape.25), calls=%async_computation.2 | async-start | bytes 524288 | tf_op jit(solution)/shard_map/all_to_all | solution.py:33
  38.1 0.6 broadcast.1
  38.6 0.9 reduce
  39.6 0.2 reshape.24
  39.8 0.2 copy.6
  39.9 0.1 stack_reshape.2
  40.1 4.6 %all-to-all-done.2 = f32[16,1,4096]{2,1,0:T(1,128)S(1)} async-done(((f32[16,1,4096]{2,1,0:T(1,128)}), f32[16,1,4096]{2,1,0:T(1,128)S(1)}, u32[]{:S(2)}, u32[]{:S(2)}) %all-to-all-start.2) | async-done | bytes 262176 | tf_op jit(solution)/shard_map/all_to_all | solution.py:33
  44.7 1.6 stack.3
  46.2 9.1 %all-to-all-start.1 = ((f32[16,32,1024]{2,1,0:T(8,128)}), f32[16,32,1024]{2,1,0:T(8,128)S(1)}, u32[]{:S(2)}, u32[]{:S(2)}) async-start(f32[16,32,1024]{2,1,0:T(8,128)} %stack.3), calls=%async_computation.1 | async-start | bytes 4194304 | tf_op jit(solution)/shard_map/all_to_all | solution.py:28
  55.4 0.0 all-gather.2.cloned.1.call-start
  55.4 1.2 reduce.1
  56.6 0.2 reshape.26
  56.9 0.3 copy.8
  57.2 0.9 reshape.22
  58.1 0.0 all-gather.2.cloned.1.call-update
  58.1 0.0 reduce-scatter.2.cloned.1.call-start
  58.1 37.9 %all-gather.2.cloned.1.call-done = f32[512,1024]{1,0:T(8,128)} async-done(((f32[64,1024]{1,0:T(8,128)}), f32[512,1024]{1,0:T(8,128)}) %all-gather.2.cloned.1.call-update) | async-done | bytes 2097168 | tf_op jit(solution)/shard_map/all_gather | solution.py:35
  96.0 0.0 all-to-all-done.1
  96.0 9.5 %fusion = f32[1024,1024]{1,0:T(8,128)} fusion(f32[512,1024]{1,0:T(8,128)S(1)} %bitcast.24, f32[512,1024]{1,0:T(8,128)} %all-gather.2.cloned.1.call-done), kind=kOutput, calls=%fused_computation.3 | convolution fusion | flops 6442450944 | bytes 8388608 | tf_op jit(solution)/shard_map/dot_general | solution.py:10
  105.5 0.0 reduce-scatter.2.cloned.1.call-update
  105.5 93.3 %reduce-scatter.2.cloned.1.call-done = f32[256,1024]{1,0:T(8,128)} async-done(((f32[1024,1024]{1,0:T(8,128)}), f32[256,1024]{1,0:T(8,128)}) %reduce-scatter.2.cloned.1.call-update) | async-done | bytes 1048592 | tf_op jit(solution)/shard_map/reduce_scatter | solution.py:36
  (1 shorter events, 0.0 us)
Async XLA Ops:
  8.6 17.8 %all-to-all-start = ((f32[8,1,4096]{2,1,0:T(1,128)}), f32[8,1,4096]{2,1,0:T(1,128)S(1)}, u32[]{:S(2)}, u32[]{:S(2)}) async-start(f32[8,1,4096]{2,1,0:T(1,128)} %reshape.23), calls=%async_computation | async-start | bytes 262144 | tf_op jit(solution)/shard_map/all_to_all | solution.py:25
  26.5 18.2 %all-to-all-start.2 = ((f32[16,1,4096]{2,1,0:T(1,128)}), f32[16,1,4096]{2,1,0:T(1,128)S(1)}, u32[]{:S(2)}, u32[]{:S(2)}) async-start(f32[16,1,4096]{2,1,0:T(1,128)} %reshape.25), calls=%async_computation.2 | async-start | bytes 524288 | tf_op jit(solution)/shard_map/all_to_all | solution.py:33
  46.2 49.8 %all-to-all-start.1 = ((f32[16,32,1024]{2,1,0:T(8,128)}), f32[16,32,1024]{2,1,0:T(8,128)S(1)}, u32[]{:S(2)}, u32[]{:S(2)}) async-start(f32[16,32,1024]{2,1,0:T(8,128)} %stack.3), calls=%async_computation.1 | async-start | bytes 4194304 | tf_op jit(solution)/shard_map/all_to_all | solution.py:28
  55.4 40.7 %all-gather.2.cloned.1.call-start = ((), (), s32[]{:S(2)}) async-start(), calls=%async_computation.4 | async-start | bytes 2359296 | tf_op jit(solution)/shard_map/all_gather | solution.py:35
  58.1 140.8 %reduce-scatter.2.cloned.1.call-start = ((), (), s32[]{:S(2)}) async-start(), calls=%async_computation.5 | async-start | bytes 5242880 | tf_op jit(solution)/shard_map/reduce_scatter | solution.py:36
Sparse Core Ops, SparseCore 0:
  58.3 37.6 all-gather.1
  105.7 93.1 reduce-scatter.1
